TPU v7x, 32 devices: a whole 2x2x4 slice. The times are simulated.
32 devices in a mesh: seq: 8 (over y, x, core), grp: 4 (over z).
Axes of the slice: x: 2, y: 2, z: 4, core: 2. Of those that a mesh axis runs over, the one named last changes fastest.
Arguments:
- tokens: bfloat16 [1024, 16, 2048], P('grp', 'seq'), may hold values from -6 to 6
- norm_gain: float32 [2048], replicated, may hold values from 0.25 to 1.75
- qk_gain: float32 [2, 2, 16, 128], P(None, None, 'grp'), may hold values from 0.5 to 12
- window_blocks: int32 [8, 4], replicated, may hold values from 0 to 7, as said below
- w_spatial: bfloat16 [2048, 3, 2048], P('seq', None, 'grp'), may hold values from -0.13258252 to 0.13258252
- w_temporal: bfloat16 [2048, 3, 2048], P('seq', None, 'grp'), may hold values from -0.13258252 to 0.13258252
- w_out: bfloat16 [2048, 2, 2048], P('seq', None, 'grp'), may hold values from -0.09375 to 0.09375
Outputs:
- block_out: bfloat16 [1024, 16, 2048], P('grp', 'seq')
Inputs may be any that keep to these rules, and one draw needn't show every extreme that they name: `window_blocks`: row t lists 4 distinct tiles, the first of them t itself.
All inputs are finite; a program needn't handle non-finite values.
Results may differ from a plain program's by a relative error of at most 0.015.
Values may be sent and summed in bfloat16 or wider, within the bound.
No kernel may reach another device: no remote copies, remote signals or barrier semaphores. Data moves between devices by JAX's collectives and lax.ppermute only.
A program may use at most 128 MiB of HBM per device.

v0:
```python
import itertools

import jax
import jax.numpy as jnp
from jax import lax
from jax.experimental import pallas as pl
from jax.experimental.pallas import tpu as pltpu
from jax.sharding import PartitionSpec as P

TILE = 128
PROJECT_WEIGHT, LIGHT_WEIGHT = 3, 10
EPS = 1e-06
VMEM_BYTES = 56 * 1024 * 1024
VMEM = pl.BlockSpec(memory_space=pltpu.VMEM)
ANY = pl.BlockSpec(memory_space=pl.ANY)
MARK = jax.ShapeDtypeStruct((8, 128), jnp.float32)


def params():
    return pltpu.CompilerParams(vmem_limit_bytes=VMEM_BYTES)


def dot_transposed(a, b):
    return lax.dot_general(a, b, (((1,), (1,)), ((), ())), preferred_element_type=jnp.float32)


class Order:
    def __init__(self):
        self.mark = None

    def call(self, kernel, operands, in_specs, out_specs, out_shape, flops, ordered=False, **more):
        count = len(operands)
        marked = ordered and self.mark is not None

        def run(*refs):
            rest = refs[count + marked :]
            kernel(*refs[:count], *rest[: len(out_shape)], *rest[len(out_shape) + ordered :])

        outs = pl.pallas_call(
            run,
            in_specs=in_specs + [ANY] * marked,
            out_specs=out_specs + [ANY] * ordered,
            out_shape=out_shape + [MARK] * ordered,
            compiler_params=params(),
            cost_estimate=pl.CostEstimate(flops=flops, bytes_accessed=0, transcendentals=0),
            **more,
        )(*operands, *([self.mark] * marked))
        if ordered:
            *outs, self.mark = outs
        return outs


def relay(order, arrays):
    return order.call(
        lambda *refs: None,
        arrays,
        [ANY] * len(arrays),
        [ANY] * len(arrays),
        [jax.ShapeDtypeStruct(x.shape, x.dtype) for x in arrays],
        0,
        ordered=True,
        input_output_aliases={i: i for i in range(len(arrays))},
        name="relay",
    )


SPATIAL, TEMPORAL = 0, 1


def project(order, tasks, weights, gains):
    arrays = []
    for _, groups in tasks:
        arrays += [x for group in groups for x in group if not any(x is y for y in arrays)]
    row_count, depth = arrays[0].shape
    split, _, _, columns = weights.shape
    heads, width = gains.shape[2], gains.shape[4]
    part = row_count // split
    together = max(1, min(heads, 256 // width))
    span = together * width

    def index(x):
        return [y is x for y in arrays].index(True)

    def branch_at(j):
        found = tasks[0][0]
        for t in range(1, len(tasks)):
            found = jnp.where(j >= 3 * t, tasks[t][0], found)
        return found

    out_shape, out_specs, writes = [], [], []
    for t, (branch, groups) in enumerate(tasks):

        def place(j, t=t):
            return jnp.clip(j - 3 * t, 0, 2)

        writes.append([])
        for g, group in enumerate(groups):
            frames = len(group)
            for f, x in enumerate(group):
                first = len(out_shape) + (f if branch == SPATIAL else 0)
                writes[-1].append((index(x), first, g, f))
            if branch == SPATIAL:
                out_shape += [jax.ShapeDtypeStruct((row_count, 3 * columns), jnp.bfloat16)] * frames
                out_specs += [
                    pl.BlockSpec((row_count, columns), lambda j, place=place: (0, place(j)))
                ] * frames
        if branch == TEMPORAL:
            whole = (split, len(groups), len(groups[0]), part, 3 * columns)
            out_shape.append(jax.ShapeDtypeStruct(whole, jnp.bfloat16))
            out_specs.append(
                pl.BlockSpec(
                    whole[:-1] + (columns,), lambda j, place=place: (0, 0, 0, 0, place(j))
                )
            )

    def kernel(*refs):
        row_refs, w_ref, gain_ref = refs[: len(arrays)], refs[len(arrays)], refs[len(arrays) + 1]
        out_refs = refs[len(arrays) + 2 :]
        step = pl.program_id(0)
        kind = step % 3

        def run(t):
            for start in range(0, heads, together):
                w = w_ref[:, :, start * width : start * width + span].reshape(depth, span)
                for source, target, g, f in writes[t]:
                    projected = jnp.dot(
                        row_refs[source][...], w, preferred_element_type=jnp.float32
                    )
                    for h in range(together):
                        one = projected[:, h * width : (h + 1) * width]
                        scale = lax.rsqrt(jnp.mean(one * one, axis=-1, keepdims=True) + EPS)
                        scale = jnp.where(kind < 2, scale, 1.0)
                        one = one * scale * gain_ref[start + h]
                        at = pl.ds((start + h) * width, width)
                        if tasks[t][0] == TEMPORAL:
                            out_refs[target][:, g, f, :, at] = one.reshape(split, part, width).astype(
                                jnp.bfloat16
                            )
                        else:
                            out_refs[target][:, at] = one.astype(jnp.bfloat16)

        for t in range(len(tasks)):
            if len(tasks) == 1:
                run(t)
            else:
                pl.when(step // 3 == t)(lambda t=t: run(t))

    outs = order.call(
        kernel,
        [*arrays, weights, gains],
        [pl.BlockSpec((row_count, depth), lambda j: (0, 0), pipeline_mode=pl.Buffered(1))]
        * len(arrays)
        + [
            pl.BlockSpec(
                (split, None, depth // split, columns),
                lambda j: (0, 3 * branch_at(j) + j % 3, 0, 0),
            ),
            pl.BlockSpec((None, None, heads, 1, width), lambda j: (branch_at(j), j % 3, 0, 0, 0)),
        ],
        out_specs,
        out_shape,
        6 * sum(map(len, writes)) * row_count * depth * columns * PROJECT_WEIGHT,
        ordered=True,
        grid=(3 * len(tasks),),
        name="project",
    )
    outs, found = list(outs), []
    for branch, groups in tasks:
        if branch == TEMPORAL:
            found.append(outs.pop(0))
        else:
            found.append([[outs.pop(0) for _ in group] for group in groups])
    return found


def temporal_attention(order, packed, heads, ordered):
    split, chunks, frames_each, patches, columns = packed.shape
    frames = split * frames_each
    width = columns // (3 * heads)
    group = min(patches, max(256 // frames, 8))
    unit = frames * group

    def kernel(x_ref, out_ref):
        row = lax.broadcasted_iota(jnp.int32, (unit, unit), 0)
        col = lax.broadcasted_iota(jnp.int32, (unit, unit), 1)
        seen = (row % group == col % group) & (col // group <= row // group)

        def read(c, first, kind, h):
            at = (kind * heads + h) * width
            piece = x_ref[:, c, :, first : first + group, at : at + width]
            if group % 16:
                return piece.astype(jnp.float32).reshape(unit, width).astype(jnp.bfloat16)
            return piece.reshape(unit, width)

        for c, first in itertools.product(range(chunks), range(0, patches, group)):
            for h in range(heads):
                q, k, v = (read(c, first, kind, h) for kind in range(3))
                scores = dot_transposed(q, k)
                scores = jnp.where(seen, scores, jnp.float32(-1e30))
                scores = jnp.exp(scores - jnp.max(scores, axis=-1, keepdims=True))
                total = jnp.sum(scores, axis=-1, keepdims=True)
                attended = jnp.dot(
                    scores.astype(jnp.bfloat16), v, preferred_element_type=jnp.float32
                )
                attended = (attended / total).reshape(split, frames_each, group, width)
                out_ref[:, c, :, first : first + group, h * width : (h + 1) * width] = (
                    attended.astype(jnp.bfloat16)
                )

    return order.call(
        kernel,
        [packed],
        [VMEM],
        [VMEM],
        [jax.ShapeDtypeStruct(packed.shape[:-1] + (heads * width,), jnp.bfloat16)],
        4 * unit * unit * width * heads * chunks * (patches // group) // LIGHT_WEIGHT,
        ordered=ordered,
        name="temporal_attention",
    )[0]


def finish_block(order, slot, frame, slots, temporal_out, w_out, table, arrived, heads, ordered):
    count = len(slots)
    row_count, columns = slots[0].shape
    columns //= 3
    width = columns // heads
    tiles_each = row_count // TILE
    listed = table.shape[1]
    split, _, depth, _ = w_out.shape
    part = temporal_out.shape[3]
    adds = arrived is not None

    def kernel(*refs):
        table_ref, slot_refs = refs[0], refs[1 : 1 + count]
        t_hbm, w_hbm = refs[1 + count], refs[2 + count]
        out_ref, q_ref, k_ref, v_ref, t_ref, w_ref, o_ref, sems = refs[3 + count + adds :][:8]

        copies = []

        def copy(source, target):
            copies.append(pltpu.make_async_copy(source, target, sems.at[len(copies)]))
            copies[-1].start()
            return copies[-1]

        first = [copy(slot_refs[slot].at[:, pl.ds(0, columns)], q_ref)]
        for s in range(count):
            at = pl.ds(s * row_count, row_count)
            first.append(copy(slot_refs[s].at[:, pl.ds(columns, columns)], k_ref.at[at]))
            first.append(copy(slot_refs[s].at[:, pl.ds(2 * columns, columns)], v_ref.at[at]))
        second = [copy(t_hbm.at[:, 0, frame], t_ref), copy(w_hbm, w_ref)]
        if adds:
            arrived_ref = refs[-1]
            second.append(copy(refs[3 + count], arrived_ref))
        for one in first:
            one.wait()
        for i in range(tiles_each):
            picks = [
                pl.ds(pl.multiple_of(table_ref[slot * tiles_each + i, j] * TILE, TILE), TILE)
                for j in range(listed)
            ]
            cuts = [pl.ds(h * width, width) for h in range(heads)]
            scores = [
                dot_transposed(
                    q_ref[pl.ds(i * TILE, TILE), at],
                    jnp.concatenate([k_ref[p, at] for p in picks], axis=0),
                )
                for at in cuts
            ]
            scores = [jnp.exp(x - jnp.max(x, axis=-1, keepdims=True)) for x in scores]
            totals = [jnp.sum(x, axis=-1, keepdims=True) for x in scores]
            for at, x, total in zip(cuts, scores, totals):
                v = jnp.concatenate([v_ref[p, at] for p in picks], axis=0)
                attended = jnp.dot(x.astype(jnp.bfloat16), v, preferred_element_type=jnp.float32)
                o_ref[pl.ds(i * TILE, TILE), at] = (attended / total).astype(jnp.bfloat16)
        for one in second:
            one.wait()
        spatial = o_ref[...]
        temporal = t_ref[...]
        if part % 16:
            temporal = temporal.astype(jnp.float32)
        temporal = temporal.reshape(row_count, columns).astype(jnp.bfloat16)
        for s in range(split):
            at = pl.ds(s * depth, depth)
            value = dot_transposed(spatial, w_ref[s, 0]) + dot_transposed(temporal, w_ref[s, 1])
            if adds:
                value += arrived_ref[:, at].astype(jnp.float32)
            out_ref[:, at] = value.astype(jnp.bfloat16)

    operands = [table, *slots, temporal_out, w_out] + [arrived] * adds
    held = (row_count, split * depth)
    scratch = [
        pltpu.VMEM((row_count, columns), jnp.bfloat16),
        pltpu.VMEM((count * row_count, columns), jnp.bfloat16),
        pltpu.VMEM((count * row_count, columns), jnp.bfloat16),
        pltpu.VMEM((split, part, columns), jnp.bfloat16),
        pltpu.VMEM((split, 2, depth, columns), jnp.bfloat16),
        pltpu.VMEM((row_count, columns), jnp.bfloat16),
        pltpu.SemaphoreType.DMA((2 * count + 4,)),
    ]
    return order.call(
        kernel,
        operands,
        [pl.BlockSpec(memory_space=pltpu.SMEM)] + [ANY] * (len(operands) - 1),
        [VMEM],
        [jax.ShapeDtypeStruct(held, jnp.bfloat16)],
        (4 * row_count * listed * TILE * columns + 4 * row_count * columns * split * depth)
        // LIGHT_WEIGHT,
        ordered=ordered,
        scratch_shapes=scratch + [pltpu.VMEM(held, jnp.bfloat16)] * adds,
        name="finish_block",
    )[0]


def combine(tokens, own, sums):
    row_count, frames, depth = tokens.shape
    block = min(row_count, 64)

    def kernel(t_ref, *refs):
        out_ref = refs[-1]
        for f in range(frames):
            total = refs[f][...].astype(jnp.float32) + refs[frames + f][...].astype(jnp.float32)
            out_ref[:, f, :] = (t_ref[:, f, :].astype(jnp.float32) + total).astype(jnp.bfloat16)

    rows = pl.BlockSpec((block, depth), lambda i: (i, 0))
    whole = pl.BlockSpec((block, frames, depth), lambda i: (i, 0, 0))
    return pl.pallas_call(
        kernel,
        grid=(row_count // block,),
        in_specs=[whole] + [rows] * (2 * frames),
        out_specs=whole,
        out_shape=jax.ShapeDtypeStruct(tokens.shape, tokens.dtype),
        compiler_params=params(),
        name="combine",
    )(tokens, *own, *sums)


def slot_order(window_blocks, me, ring, tiles_each):
    def renumber(tile):
        return (me - tile // tiles_each + ring) % ring * tiles_each + tile % tiles_each

    rows = renumber(jnp.arange(ring * tiles_each, dtype=jnp.int32))
    return renumber(window_blocks[rows])


def body(tokens, norm_gain, qk_gain, window_blocks, w_spatial, w_temporal, w_out):
    rows_here, frames_here, _ = tokens.shape
    heads, width = qk_gain.shape[2:]
    ring = lax.axis_size("grp")
    me = lax.axis_index("grp")
    forward = [(i, (i + 1) % ring) for i in range(ring)]
    order = Order()

    def send(arrays):
        return [lax.ppermute(x, "grp", forward) for x in arrays]

    def swap(array):
        return lax.all_to_all(array, "seq", split_axis=0, concat_axis=0, tiled=True)

    wide = tokens.astype(jnp.float32)
    normed = (
        wide * lax.rsqrt(jnp.mean(wide * wide, axis=-1, keepdims=True) + EPS) * norm_gain
    ).astype(jnp.bfloat16)
    full_qkv = lax.all_gather(
        jnp.concatenate([w_spatial.transpose(1, 0, 2), w_temporal.transpose(1, 0, 2)]),
        "seq",
        axis=0,
    )
    full_out = lax.all_gather(w_out.transpose(1, 0, 2), "seq", axis=0)
    gains = jnp.concatenate([qk_gain, jnp.ones_like(qk_gain[:, :1])], axis=1)
    gains = gains * jnp.array([width**-0.5, 1.0, 1.0], jnp.float32)[None, :, None, None]
    gains = gains[:, :, :, None, :]
    table = slot_order(window_blocks, me, ring, rows_here // TILE)

    def temporal(k):
        (packed,) = project(order, [(TEMPORAL, [chunks[k]])], full_qkv, gains)
        exchanged[k] = swap(packed)

    def attend(k, ordered=False):
        temporal_outs[k] = swap(temporal_attention(order, exchanged[k], heads, ordered))

    def spatial(ks):
        tasks = [(SPATIAL, [chunks[k] for k in ks])]
        slots.update(zip(ks, project(order, tasks, full_qkv, gains)[0]))

    def finish(slot, frame, arrived, ordered=False):
        return finish_block(
            order,
            slot,
            frame,
            [slots[k][frame] for k in range(ring)],
            temporal_outs[slot],
            full_out,
            table,
            arrived,
            heads,
            ordered,
        )

    last = ring - 1
    chunks = [[normed[:, f] for f in range(frames_here)]]
    chunks += [[None] * frames_here for _ in range(last)]
    slots, exchanged, temporal_outs, arrived, sums = {}, {}, {}, {}, []
    for window in range(last + frames_here - 1):
        if arrived:
            for (k, f), x in zip(arrived, relay(order, list(arrived.values()))):
                chunks[k][f] = x
        steps = [window + 1 - f for f in range(frames_here)]
        moving = [(k, f) for f, k in enumerate(steps) if 1 <= k <= last]
        arrived = {(k, f): send([chunks[k - 1][f]])[0] for k, f in moving}
        ready = window - frames_here + 1
        if ready == 1 and last > 1:
            temporal(1)
            ahead = chunks[2][: frames_here - 1] if last > 2 else []
            groups = [chunks[1], chunks[0]] + ([ahead] if ahead else [])
            found = project(order, [(SPATIAL, groups)], full_qkv, gains)[0]
            slots[1], slots[0] = found[:2]
            if ahead:
                slots[2] = found[2]
            temporal(0)
            attend(1, True)
        elif ready > 0:
            at_end = ready == last - 1
            some = chunks[last][:-1] if at_end and frames_here > 1 else []
            have = slots.setdefault(ready, [])
            tasks = [
                (SPATIAL, [chunks[ready][len(have) :]] + ([some] if some else [])),
                (TEMPORAL, [chunks[ready]]),
            ]
            found = project(order, tasks, full_qkv, gains)
            slots[ready], exchanged[ready] = have + found[0][0], swap(found[1])
            if some:
                slots[last] = found[0][1]
                sums = [finish(1, f, None, True) for f in range(len(some))]
    for (k, f), x in arrived.items():
        chunks[k][f] = x
    if last == 1:
        temporal(1)
        spatial([0])
        temporal(0)
        attend(1, True)
    have = slots.setdefault(last, [])
    tasks = [(SPATIAL, [chunks[last][len(have) :]])]
    if last > 1:
        tasks += [(TEMPORAL, [chunks[last]])]
    found = project(order, tasks, full_qkv, gains)
    have += found[0][0]
    if last > 1:
        exchanged[last] = swap(found[1])
    sums = send(sums + [finish(1, f, None, True) for f in range(len(sums), frames_here)])
    for k in range(1, ring):
        if k not in temporal_outs and k < last:
            attend(k, True)
    for k in range(ring):
        if k not in temporal_outs:
            attend(k)
    for slot in range(2, ring):
        sums = send([finish(slot, f, sums[f]) for f in range(frames_here)])
    own = [finish(0, f, None) for f in range(frames_here)]
    return combine(tokens, own, sums)


def solution(mesh):
    return jax.shard_map(
        body,
        mesh=mesh,
        in_specs=(
            P("grp", "seq", None),
            P(),
            P(None, None, "grp", None),
            P(),
            P("seq", None, "grp"),
            P("seq", None, "grp"),
            P("seq", None, "grp"),
        ),
        out_specs=P("grp", "seq", None),
        check_vma=False,
    )
```

profile of v0, /device:TPU:0, one launch (start us, length us, event | category | flops | bytes accessed | tf_op | source)
XLA Modules:
  0.0 333.1 jit_solution(12909318789367177388)
XLA Ops:
  18.7 23.5 %collective-permute-done.refs_0_ = bf16[256,2048]{1,0:T(8,128)(2,1)S(1)} collective-permute-done((bf16[256,2048]{1,0:T(8,128)(2,1)S(1)}, bf16[256,2048]{1,0:T(8,128)(2,1)S(1)}, u32[]{:S(2)}, u32[]{:S(2)}) %collective-permute-start) | collective-permute-done | bytes 1048608 | tf_op jit(solution)/shard_map/ppermute | solution.py:354
  44.5 20.1 %collective-permute-done.2.refs_1_ = bf16[256,2048]{1,0:T(8,128)(2,1)S(1)} collective-permute-done((bf16[256,2048]{1,0:T(8,128)(2,1)}, bf16[256,2048]{1,0:T(8,128)(2,1)S(1)}, u32[]{:S(2)}, u32[]{:S(2)}) %collective-permute-start.2) | collective-permute-done | bytes 1048608 | tf_op jit(solution)/shard_map/ppermute | solution.py:354
  64.6 21.6 %collective-permute-done.1.refs_0_ = bf16[256,2048]{1,0:T(8,128)(2,1)S(1)} collective-permute-done((bf16[256,2048]{1,0:T(8,128)(2,1)}, bf16[256,2048]{1,0:T(8,128)(2,1)S(1)}, u32[]{:S(2)}, u32[]{:S(2)}) %collective-permute-start.1) | collective-permute-done | bytes 1048608 | tf_op jit(solution)/shard_map/ppermute | solution.py:354
  88.5 7.7 %project.5 = (bf16[8,1,2,32,1536]{4,3,2,1,0:T(8,128)(2,1)}, f32[8,128]{1,0:T(8,128)}) custom-call(bf16[256,2048]{1,0:T(8,128)(2,1)} %get-tuple-element.37.refs_0_, bf16[256,2048]{1,0:T(8,128)(2,1)} %get-tuple-element.39.refs_1_, bf16[8,6,256,512]{3,2,1,0:T(8,128)(2,1)} %bitcast.30, f32[2,3,4,1,128]{4,3,2,1,0:T(1,128)} %bitcast.25, ...), custom_call_target="tpu_custom_call" | custom-call | flops 9663676416 | tf_op jit(solution)/shard_map/project/pallas_call | solution.py:39
  100.0 13.3 %project.6 = (bf16[256,1536]{1,0:T(8,128)(2,1)}, bf16[256,1536]{1,0:T(8,128)(2,1)}, bf16[256,1536]{1,0:T(8,128)(2,1)}, bf16[256,1536]{1,0:T(8,128)(2,1)}, bf16[256,1536]{1,0:T(8,128)(2,1)}, /*index=5*/f32[8,128]{1,0:T(8,128)}) custom-call(bf16[256,2048]{1,0:T(8,128)(2,1)} %get-tuple-element.37.refs_0_, bf16[256,2048]{1,0:T(8,128)(2,1)} %get-tuple-element.39.refs_1_, ...), custom_call_target="tpu_custom_call" | custom-call | flops 24159191040 | tf_op jit(solution)/shard_map/project/pallas_call | solution.py:39
  113.3 7.7 %project.7 = (bf16[8,1,2,32,1536]{4,3,2,1,0:T(8,128)(2,1)}, f32[8,128]{1,0:T(8,128)}) custom-call(bf16[256,2048]{1,0:T(8,128)(2,1)} %copy-done.13, bf16[256,2048]{1,0:T(8,128)(2,1)} %get-tuple-element.69.refs_3_.refs_1_, bf16[8,6,256,512]{3,2,1,0:T(8,128)(2,1)} %bitcast.32, f32[2,3,4,1,128]{4,3,2,1,0:T(1,128)} %bitcast.27, f32[8,128]{1,0:T(8,128)} %get-tuple-element.47.refs_4_), custom_call_target="tpu_custom_call" | custom-call | flops 9663676416 | tf_op jit(solution)/shard_map/project/pallas_call | solution.py:39
  121.0 6.1 %all-to-all-done.refs_0_ = bf16[8,1,2,32,1536]{4,3,2,1,0:T(8,128)(2,1)S(1)} async-done(((bf16[8,1,2,32,1536]{4,3,2,1,0:T(8,128)(2,1)}), bf16[8,1,2,32,1536]{4,3,2,1,0:T(8,128)(2,1)S(1)}, u32[]{:S(2)}, u32[]{:S(2)}) %all-to-all-start) | async-done | bytes 1572896 | tf_op jit(solution)/shard_map/all_to_all | solution.py:357
  137.7 12.9 %project.8 = (bf16[256,1536]{1,0:T(8,128)(2,1)}, bf16[256,1536]{1,0:T(8,128)(2,1)}, bf16[8,1,2,32,1536]{4,3,2,1,0:T(8,128)(2,1)}, f32[8,128]{1,0:T(8,128)}) custom-call(bf16[256,2048]{1,0:T(8,128)(2,1)} %get-tuple-element.50.refs_0_, bf16[256,2048]{1,0:T(8,128)(2,1)} %get-tuple-element.51.refs_1_, bf16[256,2048]{1,0:T(8,128)(2,1)} %get-tuple-element.40.refs_4_.refs_2_, ...), custom_call_target="tpu_custom_call" | custom-call | flops 19327352832 | tf_op jit(solution)/shard_map/project/pallas_call | solution.py:39
  155.4 6.1 %finish_block.9 = (bf16[256,2048]{1,0:T(8,128)(2,1)}, f32[8,128]{1,0:T(8,128)}) custom-call(s32[8,4]{1,0:T(8,128)} %fusion.7.refs_0_, bf16[256,1536]{1,0:T(8,128)(2,1)} %get-tuple-element.43.refs_1_, bf16[256,1536]{1,0:T(8,128)(2,1)} %get-tuple-element.44.refs_2_, bf16[256,1536]{1,0:T(8,128)(2,1)} %get-tuple-element.45.refs_3_, ...), custom_call_target="tpu_custom_call" | custom-call | flops 134217728 | tf_op jit(solution)/shard_map/finish_block/pallas_call | solution.py:39
  164.5 11.4 %project.9 = (bf16[256,1536]{1,0:T(8,128)(2,1)}, bf16[8,1,2,32,1536]{4,3,2,1,0:T(8,128)(2,1)}, f32[8,128]{1,0:T(8,128)}) custom-call(bf16[256,2048]{1,0:T(8,128)(2,1)} %copy-done.20, bf16[256,2048]{1,0:T(8,128)(2,1)} %get-tuple-element.51.refs_1_, bf16[8,6,256,512]{3,2,1,0:T(8,128)(2,1)} %bitcast.34, f32[2,3,4,1,128]{4,3,2,1,0:T(1,128)} %bitcast.29, ...), custom_call_target="tpu_custom_call" | custom-call | flops 14495514624 | tf_op jit(solution)/shard_map/project/pallas_call | solution.py:39
  182.3 6.1 %finish_block.11 = (bf16[256,2048]{1,0:T(8,128)(2,1)}, f32[8,128]{1,0:T(8,128)}) custom-call(s32[8,4]{1,0:T(8,128)} %fusion.7.refs_0_, bf16[256,1536]{1,0:T(8,128)(2,1)} %get-tuple-element.55.refs_1_, bf16[256,1536]{1,0:T(8,128)(2,1)} %get-tuple-element.56.refs_2_, bf16[256,1536]{1,0:T(8,128)(2,1)} %get-tuple-element.57.refs_3_, ...), custom_call_target="tpu_custom_call" | custom-call | flops 134217728 | tf_op jit(solution)/shard_map/finish_block/pallas_call | solution.py:39
  192.1 8.8 %all-to-all-done.4.refs_0_ = bf16[8,1,2,32,1536]{4,3,2,1,0:T(8,128)(2,1)S(1)} async-done(((bf16[8,1,2,32,1536]{4,3,2,1,0:T(8,128)(2,1)}), bf16[8,1,2,32,1536]{4,3,2,1,0:T(8,128)(2,1)S(1)}, u32[]{:S(2)}, u32[]{:S(2)}) %all-to-all-start.4) | async-done | bytes 1572896 | tf_op jit(solution)/shard_map/all_to_all | solution.py:357
  207.8 6.3 %all-to-all-done.7.refs_5_ = bf16[8,1,2,32,512]{4,3,2,1,0:T(8,128)(2,1)S(1)} async-done(((bf16[8,1,2,32,512]{4,3,2,1,0:T(8,128)(2,1)}), bf16[8,1,2,32,512]{4,3,2,1,0:T(8,128)(2,1)S(1)}, u32[]{:S(2)}, u32[]{:S(2)}) %all-to-all-start.7) | async-done | bytes 524320 | tf_op jit(solution)/shard_map/all_to_all | solution.py:357
  217.8 6.3 %finish_block.12 = bf16[256,2048]{1,0:T(8,128)(2,1)} custom-call(s32[8,4]{1,0:T(8,128)} %fusion.7.refs_0_, bf16[256,1536]{1,0:T(8,128)(2,1)} %get-tuple-element.43.refs_1_, bf16[256,1536]{1,0:T(8,128)(2,1)} %get-tuple-element.44.refs_2_, bf16[256,1536]{1,0:T(8,128)(2,1)} %get-tuple-element.45.refs_3_, bf16[256,1536]{1,0:T(8,128)(2,1)} %get-tuple-element.53.refs_4_, ...), custom_call_target="tpu_custom_call" | custom-call | flops 134217728 | tf_op jit(solution)/shard_map/finish_block/pallas_call | solution.py:39
  230.4 6.4 %finish_block.14 = bf16[256,2048]{1,0:T(8,128)(2,1)} custom-call(s32[8,4]{1,0:T(8,128)} %fusion.7.refs_0_, bf16[256,1536]{1,0:T(8,128)(2,1)} %get-tuple-element.55.refs_1_, bf16[256,1536]{1,0:T(8,128)(2,1)} %get-tuple-element.56.refs_2_, bf16[256,1536]{1,0:T(8,128)(2,1)} %get-tuple-element.57.refs_3_, bf16[256,1536]{1,0:T(8,128)(2,1)} %get-tuple-element.61.refs_4_, ...), custom_call_target="tpu_custom_call" | custom-call | flops 134217728 | tf_op jit(solution)/shard_map/finish_block/pallas_call | solution.py:39
  241.6 11.2 %collective-permute-done.7.refs_7_ = bf16[256,2048]{1,0:T(8,128)(2,1)S(1)} collective-permute-done((bf16[256,2048]{1,0:T(8,128)(2,1)}, bf16[256,2048]{1,0:T(8,128)(2,1)S(1)}, u32[]{:S(2)}, u32[]{:S(2)}) %collective-permute-start.7) | collective-permute-done | bytes 1048608 | tf_op jit(solution)/shard_map/ppermute | solution.py:354
  253.8 6.3 %finish_block.13 = bf16[256,2048]{1,0:T(8,128)(2,1)} custom-call(s32[8,4]{1,0:T(8,128)} %fusion.7.refs_0_, bf16[256,1536]{1,0:T(8,128)(2,1)} %get-tuple-element.43.refs_1_, bf16[256,1536]{1,0:T(8,128)(2,1)} %get-tuple-element.44.refs_2_, bf16[256,1536]{1,0:T(8,128)(2,1)} %get-tuple-element.45.refs_3_, bf16[256,1536]{1,0:T(8,128)(2,1)} %get-tuple-element.53.refs_4_, ...), custom_call_target="tpu_custom_call" | custom-call | flops 134217728 | tf_op jit(solution)/shard_map/finish_block/pallas_call | solution.py:39
  260.7 14.6 %collective-permute-done.10.refs_7_ = bf16[256,2048]{1,0:T(8,128)(2,1)} collective-permute-done((bf16[256,2048]{1,0:T(8,128)(2,1)}, bf16[256,2048]{1,0:T(8,128)(2,1)}, u32[]{:S(2)}, u32[]{:S(2)}) %collective-permute-start.10) | collective-permute-done | bytes 1048608 | tf_op jit(solution)/shard_map/ppermute | solution.py:354
  275.4 6.3 %finish_block.15 = bf16[256,2048]{1,0:T(8,128)(2,1)} custom-call(s32[8,4]{1,0:T(8,128)} %fusion.7.refs_0_, bf16[256,1536]{1,0:T(8,128)(2,1)} %get-tuple-element.55.refs_1_, bf16[256,1536]{1,0:T(8,128)(2,1)} %get-tuple-element.56.refs_2_, bf16[256,1536]{1,0:T(8,128)(2,1)} %get-tuple-element.57.refs_3_, bf16[256,1536]{1,0:T(8,128)(2,1)} %get-tuple-element.61.refs_4_, ...), custom_call_target="tpu_custom_call" | custom-call | flops 134217728 | tf_op jit(solution)/shard_map/finish_block/pallas_call | solution.py:39
  286.9 14.0 %all_to_all.40.refs_5_ = bf16[8,1,2,32,512]{4,3,2,1,0:T(8,128)(2,1)} all-to-all(bf16[8,1,2,32,512]{4,3,2,1,0:T(8,128)(2,1)} %temporal_attention.5), channel_id=1, replica_groups=mesh['seq'=8,'grp'=4] {'seq'}, dimensions={0} | all-to-all | bytes 1048576 | tf_op jit(solution)/shard_map/all_to_all | solution.py:357
  300.8 6.1 %finish_block.8.refs_0_ = bf16[256,2048]{1,0:T(8,128)(2,1)} custom-call(s32[8,4]{1,0:T(8,128)} %fusion.7.refs_0_, bf16[256,1536]{1,0:T(8,128)(2,1)} %get-tuple-element.43.refs_1_, bf16[256,1536]{1,0:T(8,128)(2,1)} %get-tuple-element.44.refs_2_, bf16[256,1536]{1,0:T(8,128)(2,1)} %get-tuple-element.45.refs_3_, bf16[256,1536]{1,0:T(8,128)(2,1)} %get-tuple-element.53.refs_4_, ...), custom_call_target="tpu_custom_call" | custom-call | flops 134217728 | tf_op jit(solution)/shard_map/finish_block/pallas_call | solution.py:39
  306.9 6.1 %finish_block.10.refs_1_ = bf16[256,2048]{1,0:T(8,128)(2,1)} custom-call(s32[8,4]{1,0:T(8,128)} %fusion.7.refs_0_, bf16[256,1536]{1,0:T(8,128)(2,1)} %get-tuple-element.55.refs_1_, bf16[256,1536]{1,0:T(8,128)(2,1)} %get-tuple-element.56.refs_2_, bf16[256,1536]{1,0:T(8,128)(2,1)} %get-tuple-element.57.refs_3_, bf16[256,1536]{1,0:T(8,128)(2,1)} %get-tuple-element.61.refs_4_, ...), custom_call_target="tpu_custom_call" | custom-call | flops 134217728 | tf_op jit(solution)/shard_map/finish_block/pallas_call | solution.py:39
  313.1 6.9 %collective-permute-done.11.refs_3_ = bf16[256,2048]{1,0:T(8,128)(2,1)} collective-permute-done((bf16[256,2048]{1,0:T(8,128)(2,1)}, bf16[256,2048]{1,0:T(8,128)(2,1)}, u32[]{:S(2)}, u32[]{:S(2)}) %collective-permute-start.11) | collective-permute-done | bytes 1048608 | tf_op jit(solution)/shard_map/ppermute | solution.py:354
  319.9 6.4 %combine.1 = bf16[256,2,2048]{2,1,0:T(2,128)(2,1)} custom-call(bf16[256,2,2048]{2,1,0:T(2,128)(2,1)} %t_ref.1, bf16[256,2048]{1,0:T(8,128)(2,1)} %finish_block.8.refs_0_, bf16[256,2048]{1,0:T(8,128)(2,1)} %finish_block.10.refs_1_, bf16[256,2048]{1,0:T(8,128)(2,1)} %copy-done.14, bf16[256,2048]{1,0:T(8,128)(2,1)} %collective-permute-done.11.refs_3_), custom_call_target="tpu_custom_call" | custom-call | tf_op jit(solution)/shard_map/combine/pallas_call | solution.py:326
  (96 shorter events, 77.1 us)
Async XLA Ops:
  6.5 82.0 %all-gather.5.cloned.1.call-start = ((), (), s32[]{:S(2)}) async-start(), calls=%async_computation.8 | async-start | bytes 14155776 | tf_op jit(solution)/shard_map/all_gather | solution.py:363
  9.4 146.0 %all-gather.7.cloned.1.call-start = ((), (), s32[]{:S(2)}) async-start(), calls=%async_computation.9 | async-start | bytes 4718592 | tf_op jit(solution)/shard_map/all_gather | solution.py:368
  13.0 30.1 %copy-start.18 = (s32[8,4]{0,1:T(4,128)S(1)}, s32[8,4]{0,1:T(4,128)}, u32[]{:S(2)}) copy-start(s32[8,4]{0,1:T(4,128)} %param.11) | copy-start | bytes 388
  13.0 30.8 %copy-start.17 = (f32[2,2,4,128]{3,2,1,0:T(4,128)S(1)}, f32[2,2,4,128]{3,2,1,0:T(4,128)}, u32[]{:S(2)}) copy-start(f32[2,2,4,128]{3,2,1,0:T(4,128)} %param.10) | copy-start | bytes 24580
  13.0 30.8 %copy-start.19 = (f32[3]{0:T(128)S(1)}, f32[3]{0:T(128)}, u32[]{:S(2)}) copy-start(f32[3]{0:T(128)} %constant.84.clone) | copy-start | bytes 40
  13.0 29.1 %collective-permute-start = (bf16[256,2048]{1,0:T(8,128)(2,1)S(1)}, bf16[256,2048]{1,0:T(8,128)(2,1)S(1)}, u32[]{:S(2)}, u32[]{:S(2)}) collective-permute-start(bf16[256,2048]{1,0:T(8,128)(2,1)S(1)} %get-tuple-element.70.refs_2_.refs_0_), channel_id=1, source_target_pairs={{0,1},{1,2},{2,3},{3,0},{4,5},{5,6},{6,7},{7,4},{8,9},{9,10},{10,1... | collective-permute-start | bytes 3145736 | tf_op jit(solution)/shard_map/ppermute | solution.py:354
  17.0 47.6 %collective-permute-start.2 = (bf16[256,2048]{1,0:T(8,128)(2,1)}, bf16[256,2048]{1,0:T(8,128)(2,1)S(1)}, u32[]{:S(2)}, u32[]{:S(2)}) collective-permute-start(bf16[256,2048]{1,0:T(8,128)(2,1)} %get-tuple-element.69.refs_3_.refs_1_), channel_id=1, source_target_pairs={{0,1},{1,2},{2,3},{3,0},{4,5},{5,6},{6,7},{7,4},{8,9},{9,10},{10,1... | collective-permute-start | bytes 3145736 | tf_op jit(solution)/shard_map/ppermute | solution.py:354
  43.1 43.1 %collective-permute-start.1 = (bf16[256,2048]{1,0:T(8,128)(2,1)}, bf16[256,2048]{1,0:T(8,128)(2,1)S(1)}, u32[]{:S(2)}, u32[]{:S(2)}) collective-permute-start(bf16[256,2048]{1,0:T(8,128)(2,1)} %get-tuple-element.37.refs_0_), channel_id=1, source_target_pairs={{0,1},{1,2},{2,3},{3,0},{4,5},{5,6},{6,7},{7,4},{8,9},{9,10},{10,1... | collective-permute-start | bytes 3145736 | tf_op jit(solution)/shard_map/ppermute | solution.py:354
  87.2 47.8 %collective-permute-start.4 = (bf16[256,2048]{1,0:T(8,128)(2,1)}, bf16[256,2048]{1,0:T(8,128)(2,1)S(1)}, u32[]{:S(2)}, u32[]{:S(2)}) collective-permute-start(bf16[256,2048]{1,0:T(8,128)(2,1)} %get-tuple-element.39.refs_1_), channel_id=1, source_target_pairs={{0,1},{1,2},{2,3},{3,0},{4,5},{5,6},{6,7},{7,4},{8,9},{9,10},{10,1... | collective-permute-start | bytes 3145736 | tf_op jit(solution)/shard_map/ppermute | solution.py:354
  87.2 48.9 %collective-permute-start.3 = (bf16[256,2048]{1,0:T(8,128)(2,1)}, bf16[256,2048]{1,0:T(8,128)(2,1)}, u32[]{:S(2)}, u32[]{:S(2)}) collective-permute-start(bf16[256,2048]{1,0:T(8,128)(2,1)} %get-tuple-element.40.refs_4_.refs_2_), channel_id=1, source_target_pairs={{0,1},{1,2},{2,3},{3,0},{4,5},{5,6},{6,7},{7,4},{8,9},{9,10},{10,1... | collective-permute-start | bytes 3145736 | tf_op jit(solution)/shard_map/ppermute | solution.py:354
  96.3 30.8 %all-to-all-start = ((bf16[8,1,2,32,1536]{4,3,2,1,0:T(8,128)(2,1)}), bf16[8,1,2,32,1536]{4,3,2,1,0:T(8,128)(2,1)S(1)}, u32[]{:S(2)}, u32[]{:S(2)}) async-start(bf16[8,1,2,32,1536]{4,3,2,1,0:T(8,128)(2,1)} %get-tuple-element.46), calls=%async_computation | async-start | bytes 3145728 | tf_op jit(solution)/shard_map/all_to_all | solution.py:357
  131.6 19.1 %all-to-all-start.3 = ((bf16[8,1,2,32,512]{4,3,2,1,0:T(8,128)(2,1)}), bf16[8,1,2,32,512]{4,3,2,1,0:T(8,128)(2,1)S(1)}, u32[]{:S(2)}, u32[]{:S(2)}) async-start(bf16[8,1,2,32,512]{4,3,2,1,0:T(8,128)(2,1)} %get-tuple-element.58), calls=%async_computation.3 | async-start | bytes 1048576 | tf_op jit(solution)/shard_map/all_to_all | solution.py:357
  136.2 27.4 %collective-permute-start.5 = (bf16[256,2048]{1,0:T(8,128)(2,1)}, bf16[256,2048]{1,0:T(8,128)(2,1)S(1)}, u32[]{:S(2)}, u32[]{:S(2)}) collective-permute-start(bf16[256,2048]{1,0:T(8,128)(2,1)} %get-tuple-element.50.refs_0_), channel_id=1, source_target_pairs={{0,1},{1,2},{2,3},{3,0},{4,5},{5,6},{6,7},{7,4},{8,9},{9,10},{10,1... | collective-permute-start | bytes 3145736 | tf_op jit(solution)/shard_map/ppermute | solution.py:354
  150.6 25.3 %all-to-all-start.6 = ((bf16[8,1,2,32,1536]{4,3,2,1,0:T(8,128)(2,1)}), bf16[8,1,2,32,1536]{4,3,2,1,0:T(8,128)(2,1)S(1)}, u32[]{:S(2)}, u32[]{:S(2)}) async-start(bf16[8,1,2,32,1536]{4,3,2,1,0:T(8,128)(2,1)} %get-tuple-element.63), calls=%async_computation.6 | async-start | bytes 3145728 | tf_op jit(solution)/shard_map/all_to_all | solution.py:357
  176.0 24.9 %all-to-all-start.4 = ((bf16[8,1,2,32,1536]{4,3,2,1,0:T(8,128)(2,1)}), bf16[8,1,2,32,1536]{4,3,2,1,0:T(8,128)(2,1)S(1)}, u32[]{:S(2)}, u32[]{:S(2)}) async-start(bf16[8,1,2,32,1536]{4,3,2,1,0:T(8,128)(2,1)} %get-tuple-element.62), calls=%async_computation.4 | async-start | bytes 3145728 | tf_op jit(solution)/shard_map/all_to_all | solution.py:357
  179.9 37.9 %collective-permute-start.6 = (bf16[256,2048]{1,0:T(8,128)(2,1)}, bf16[256,2048]{1,0:T(8,128)(2,1)}, u32[]{:S(2)}, u32[]{:S(2)}) collective-permute-start(bf16[256,2048]{1,0:T(8,128)(2,1)} %get-tuple-element.67), channel_id=1, source_target_pairs={{0,1},{1,2},{2,3},{3,0},{4,5},{5,6},{6,7},{7,4},{8,9},{9,10},{10,1... | collective-permute-start | bytes 3145736 | tf_op jit(solution)/shard_map/ppermute | solution.py:354
  188.4 42.0 %collective-permute-start.9 = (bf16[256,2048]{1,0:T(8,128)(2,1)}, bf16[256,2048]{1,0:T(8,128)(2,1)}, u32[]{:S(2)}, u32[]{:S(2)}) collective-permute-start(bf16[256,2048]{1,0:T(8,128)(2,1)} %get-tuple-element.68), channel_id=1, source_target_pairs={{0,1},{1,2},{2,3},{3,0},{4,5},{5,6},{6,7},{7,4},{8,9},{9,10},{10,1... | collective-permute-start | bytes 3145736 | tf_op jit(solution)/shard_map/ppermute | solution.py:354
  200.9 13.2 %all-to-all-start.7 = ((bf16[8,1,2,32,512]{4,3,2,1,0:T(8,128)(2,1)}), bf16[8,1,2,32,512]{4,3,2,1,0:T(8,128)(2,1)S(1)}, u32[]{:S(2)}, u32[]{:S(2)}) async-start(bf16[8,1,2,32,512]{4,3,2,1,0:T(8,128)(2,1)} %get-tuple-element.66), calls=%async_computation.7 | async-start | bytes 1048576 | tf_op jit(solution)/shard_map/all_to_all | solution.py:357
  214.1 23.4 %all-to-all-start.5 = ((bf16[8,1,2,32,512]{4,3,2,1,0:T(8,128)(2,1)}), bf16[8,1,2,32,512]{4,3,2,1,0:T(8,128)(2,1)S(1)}, u32[]{:S(2)}, u32[]{:S(2)}) async-start(bf16[8,1,2,32,512]{4,3,2,1,0:T(8,128)(2,1)} %temporal_attention.6), calls=%async_computation.5 | async-start | bytes 1048576 | tf_op jit(solution)/shard_map/all_to_all | solution.py:357
  224.2 28.6 %collective-permute-start.7 = (bf16[256,2048]{1,0:T(8,128)(2,1)}, bf16[256,2048]{1,0:T(8,128)(2,1)S(1)}, u32[]{:S(2)}, u32[]{:S(2)}) collective-permute-start(bf16[256,2048]{1,0:T(8,128)(2,1)} %finish_block.12), channel_id=1, source_target_pairs={{0,1},{1,2},{2,3},{3,0},{4,5},{5,6},{6,7},{7,4},{8,9},{9,10},{10,1... | collective-permute-start | bytes 3145736 | tf_op jit(solution)/shard_map/ppermute | solution.py:354
  236.8 38.6 %collective-permute-start.10 = (bf16[256,2048]{1,0:T(8,128)(2,1)}, bf16[256,2048]{1,0:T(8,128)(2,1)}, u32[]{:S(2)}, u32[]{:S(2)}) collective-permute-start(bf16[256,2048]{1,0:T(8,128)(2,1)} %finish_block.14), channel_id=1, source_target_pairs={{0,1},{1,2},{2,3},{3,0},{4,5},{5,6},{6,7},{7,4},{8,9},{9,10},{10,1... | collective-permute-start | bytes 3145736 | tf_op jit(solution)/shard_map/ppermute | solution.py:354
  237.5 44.9 %all-to-all-start.1 = ((bf16[8,1,2,32,1536]{4,3,2,1,0:T(8,128)(2,1)}), bf16[8,1,2,32,1536]{4,3,2,1,0:T(8,128)(2,1)S(1)}, u32[]{:S(2)}, u32[]{:S(2)}) async-start(bf16[8,1,2,32,1536]{4,3,2,1,0:T(8,128)(2,1)} %get-tuple-element.54), calls=%async_computation.1 | async-start | bytes 3145728 | tf_op jit(solution)/shard_map/all_to_all | solution.py:357
  260.1 53.0 %collective-permute-start.8 = (bf16[256,2048]{1,0:T(8,128)(2,1)}, bf16[256,2048]{1,0:T(8,128)(2,1)S(1)}, u32[]{:S(2)}, u32[]{:S(2)}) collective-permute-start(bf16[256,2048]{1,0:T(8,128)(2,1)} %finish_block.13), channel_id=1, source_target_pairs={{0,1},{1,2},{2,3},{3,0},{4,5},{5,6},{6,7},{7,4},{8,9},{9,10},{10,1... | collective-permute-start | bytes 3145736 | tf_op jit(solution)/shard_map/ppermute | solution.py:354
  281.7 38.2 %collective-permute-start.11 = (bf16[256,2048]{1,0:T(8,128)(2,1)}, bf16[256,2048]{1,0:T(8,128)(2,1)}, u32[]{:S(2)}, u32[]{:S(2)}) collective-permute-start(bf16[256,2048]{1,0:T(8,128)(2,1)} %finish_block.15), channel_id=1, source_target_pairs={{0,1},{1,2},{2,3},{3,0},{4,5},{5,6},{6,7},{7,4},{8,9},{9,10},{10,1... | collective-permute-start | bytes 3145736 | tf_op jit(solution)/shard_map/ppermute | solution.py:354
  (18 other events, 114.1 us)
Sparse Core Ops, SparseCore 0:
  9.5 74.8 all-gather.4
  86.2 46.7 all-gather.6
where the time goes:
time: 335 us; the launch traced here: 333 us
  waiting for transfers between devices  126 us (38%)
  Pallas kernels  123 us (37%)
  starting transfers between devices  41.2 us (12%)
  blocking collectives  14 us (4%)
  between operations  13.7 us (4%)
  local copies, waits for them, and re-layouts  9.01 us (3%)
  other arithmetic  6.47 us (2%)
    pallas_call x20, Pallas kernels, call(): pl.pallas_call(run, in_specs=in_specs + [ANY] * marked, out_specs=out_spe...  116 us
    ppermute x12, waiting for transfers between devices, send(): return [lax.ppermute(x, 'grp', forward) for x in arrays]  105 us
    all_to_all x7, starting transfers between devices, swap(): return lax.all_to_all(array, 'seq', split_axis=0, concat_axis=0, tiled=True)  26.5 us
    all_to_all x7, waiting for transfers between devices, swap(): return lax.all_to_all(array, 'seq', split_axis=0, concat_axis=0, tiled=True)  21.3 us
    ppermute x12, starting transfers between devices, send(): return [lax.ppermute(x, 'grp', forward) for x in arrays]  14.6 us
    all_to_all x1, blocking collectives, swap(): return lax.all_to_all(array, 'seq', split_axis=0, concat_axis=0, tiled=True)  14 us
    unnamed x44, local copies, waits for them, and re-layouts  7.25 us
  transfers between devices with their start and end apart: 21, of which 12 were waited for; matrix products, arithmetic and copies ran while one was open for 2% of the time, Pallas kernels for 35%

commit v1 on v0

--- a/solution.py
+++ b/solution.py
@@ -313,7 +313,7 @@
 
 def combine(tokens, own, sums):
     row_count, frames, depth = tokens.shape
-    block = min(row_count, 64)
+    block = min(row_count, 32)
 
     def kernel(t_ref, *refs):
         out_ref = refs[-1]

time: 335 us -> 336 us (level)
  no operation moved by 1% of the time
where the time goes in v1:
time: 336 us; the launch traced here: 334 us
  waiting for transfers between devices  126 us (38%)
  Pallas kernels  124 us (37%)
  starting transfers between devices  41.2 us (12%)
  blocking collectives  14 us (4%)
  between operations  13.7 us (4%)
  local copies, waits for them, and re-layouts  9.01 us (3%)
  other arithmetic  6.47 us (2%)
    pallas_call x20, Pallas kernels, call(): pl.pallas_call(run, in_specs=in_specs + [ANY] * marked, out_specs=out_spe...  116 us
    ppermute x12, waiting for transfers between devices, send(): return [lax.ppermute(x, 'grp', forward) for x in arrays]  105 us
    all_to_all x7, starting transfers between devices, swap(): return lax.all_to_all(array, 'seq', split_axis=0, concat_axis=0, tiled=True)  26.5 us
    all_to_all x7, waiting for transfers between devices, swap(): return lax.all_to_all(array, 'seq', split_axis=0, concat_axis=0, tiled=True)  21.3 us
    ppermute x12, starting transfers between devices, send(): return [lax.ppermute(x, 'grp', forward) for x in arrays]  14.6 us
    all_to_all x1, blocking collectives, swap(): return lax.all_to_all(array, 'seq', split_axis=0, concat_axis=0, tiled=True)  14 us
    pallas_call x1, Pallas kernels, combine(): pl.pallas_call(kernel, grid=(row_count // block,), in_specs=[whole] + [ro...  7.72 us
    unnamed x44, local copies, waits for them, and re-layouts  7.25 us
  transfers between devices with their start and end apart: 21, of which 12 were waited for; matrix products, arithmetic and copies ran while one was open for 2% of the time, Pallas kernels for 35%

profile of v1, /device:TPU:0, one launch (start us, length us, event | category | flops | bytes accessed | tf_op | source)
XLA Modules:
  0.0 334.5 jit_solution(13857335528242632331)
XLA Ops:
  18.7 23.5 %collective-permute-done.refs_0_ = bf16[256,2048]{1,0:T(8,128)(2,1)S(1)} collective-permute-done((bf16[256,2048]{1,0:T(8,128)(2,1)S(1)}, bf16[256,2048]{1,0:T(8,128)(2,1)S(1)}, u32[]{:S(2)}, u32[]{:S(2)}) %collective-permute-start) | collective-permute-done | bytes 1048608 | tf_op jit(solution)/shard_map/ppermute | solution.py:354
  44.5 20.1 %collective-permute-done.2.refs_1_ = bf16[256,2048]{1,0:T(8,128)(2,1)S(1)} collective-permute-done((bf16[256,2048]{1,0:T(8,128)(2,1)}, bf16[256,2048]{1,0:T(8,128)(2,1)S(1)}, u32[]{:S(2)}, u32[]{:S(2)}) %collective-permute-start.2) | collective-permute-done | bytes 1048608 | tf_op jit(solution)/shard_map/ppermute | solution.py:354
  64.6 21.6 %collective-permute-done.1.refs_0_ = bf16[256,2048]{1,0:T(8,128)(2,1)S(1)} collective-permute-done((bf16[256,2048]{1,0:T(8,128)(2,1)}, bf16[256,2048]{1,0:T(8,128)(2,1)S(1)}, u32[]{:S(2)}, u32[]{:S(2)}) %collective-permute-start.1) | collective-permute-done | bytes 1048608 | tf_op jit(solution)/shard_map/ppermute | solution.py:354
  88.5 7.7 %project.5 = (bf16[8,1,2,32,1536]{4,3,2,1,0:T(8,128)(2,1)}, f32[8,128]{1,0:T(8,128)}) custom-call(bf16[256,2048]{1,0:T(8,128)(2,1)} %get-tuple-element.37.refs_0_, bf16[256,2048]{1,0:T(8,128)(2,1)} %get-tuple-element.39.refs_1_, bf16[8,6,256,512]{3,2,1,0:T(8,128)(2,1)} %bitcast.30, f32[2,3,4,1,128]{4,3,2,1,0:T(1,128)} %bitcast.25, ...), custom_call_target="tpu_custom_call" | custom-call | flops 9663676416 | tf_op jit(solution)/shard_map/project/pallas_call | solution.py:39
  100.0 13.3 %project.6 = (bf16[256,1536]{1,0:T(8,128)(2,1)}, bf16[256,1536]{1,0:T(8,128)(2,1)}, bf16[256,1536]{1,0:T(8,128)(2,1)}, bf16[256,1536]{1,0:T(8,128)(2,1)}, bf16[256,1536]{1,0:T(8,128)(2,1)}, /*index=5*/f32[8,128]{1,0:T(8,128)}) custom-call(bf16[256,2048]{1,0:T(8,128)(2,1)} %get-tuple-element.37.refs_0_, bf16[256,2048]{1,0:T(8,128)(2,1)} %get-tuple-element.39.refs_1_, ...), custom_call_target="tpu_custom_call" | custom-call | flops 24159191040 | tf_op jit(solution)/shard_map/project/pallas_call | solution.py:39
  113.3 7.7 %project.7 = (bf16[8,1,2,32,1536]{4,3,2,1,0:T(8,128)(2,1)}, f32[8,128]{1,0:T(8,128)}) custom-call(bf16[256,2048]{1,0:T(8,128)(2,1)} %copy-done.13, bf16[256,2048]{1,0:T(8,128)(2,1)} %get-tuple-element.69.refs_3_.refs_1_, bf16[8,6,256,512]{3,2,1,0:T(8,128)(2,1)} %bitcast.32, f32[2,3,4,1,128]{4,3,2,1,0:T(1,128)} %bitcast.27, f32[8,128]{1,0:T(8,128)} %get-tuple-element.47.refs_4_), custom_call_target="tpu_custom_call" | custom-call | flops 9663676416 | tf_op jit(solution)/shard_map/project/pallas_call | solution.py:39
  121.0 6.1 %all-to-all-done.refs_0_ = bf16[8,1,2,32,1536]{4,3,2,1,0:T(8,128)(2,1)S(1)} async-done(((bf16[8,1,2,32,1536]{4,3,2,1,0:T(8,128)(2,1)}), bf16[8,1,2,32,1536]{4,3,2,1,0:T(8,128)(2,1)S(1)}, u32[]{:S(2)}, u32[]{:S(2)}) %all-to-all-start) | async-done | bytes 1572896 | tf_op jit(solution)/shard_map/all_to_all | solution.py:357
  137.7 12.9 %project.8 = (bf16[256,1536]{1,0:T(8,128)(2,1)}, bf16[256,1536]{1,0:T(8,128)(2,1)}, bf16[8,1,2,32,1536]{4,3,2,1,0:T(8,128)(2,1)}, f32[8,128]{1,0:T(8,128)}) custom-call(bf16[256,2048]{1,0:T(8,128)(2,1)} %get-tuple-element.50.refs_0_, bf16[256,2048]{1,0:T(8,128)(2,1)} %get-tuple-element.51.refs_1_, bf16[256,2048]{1,0:T(8,128)(2,1)} %get-tuple-element.40.refs_4_.refs_2_, ...), custom_call_target="tpu_custom_call" | custom-call | flops 19327352832 | tf_op jit(solution)/shard_map/project/pallas_call | solution.py:39
  155.4 6.1 %finish_block.9 = (bf16[256,2048]{1,0:T(8,128)(2,1)}, f32[8,128]{1,0:T(8,128)}) custom-call(s32[8,4]{1,0:T(8,128)} %fusion.7.refs_0_, bf16[256,1536]{1,0:T(8,128)(2,1)} %get-tuple-element.43.refs_1_, bf16[256,1536]{1,0:T(8,128)(2,1)} %get-tuple-element.44.refs_2_, bf16[256,1536]{1,0:T(8,128)(2,1)} %get-tuple-element.45.refs_3_, ...), custom_call_target="tpu_custom_call" | custom-call | flops 134217728 | tf_op jit(solution)/shard_map/finish_block/pallas_call | solution.py:39
  164.5 11.4 %project.9 = (bf16[256,1536]{1,0:T(8,128)(2,1)}, bf16[8,1,2,32,1536]{4,3,2,1,0:T(8,128)(2,1)}, f32[8,128]{1,0:T(8,128)}) custom-call(bf16[256,2048]{1,0:T(8,128)(2,1)} %copy-done.20, bf16[256,2048]{1,0:T(8,128)(2,1)} %get-tuple-element.51.refs_1_, bf16[8,6,256,512]{3,2,1,0:T(8,128)(2,1)} %bitcast.34, f32[2,3,4,1,128]{4,3,2,1,0:T(1,128)} %bitcast.29, ...), custom_call_target="tpu_custom_call" | custom-call | flops 14495514624 | tf_op jit(solution)/shard_map/project/pallas_call | solution.py:39
  182.3 6.1 %finish_block.11 = (bf16[256,2048]{1,0:T(8,128)(2,1)}, f32[8,128]{1,0:T(8,128)}) custom-call(s32[8,4]{1,0:T(8,128)} %fusion.7.refs_0_, bf16[256,1536]{1,0:T(8,128)(2,1)} %get-tuple-element.55.refs_1_, bf16[256,1536]{1,0:T(8,128)(2,1)} %get-tuple-element.56.refs_2_, bf16[256,1536]{1,0:T(8,128)(2,1)} %get-tuple-element.57.refs_3_, ...), custom_call_target="tpu_custom_call" | custom-call | flops 134217728 | tf_op jit(solution)/shard_map/finish_block/pallas_call | solution.py:39
  192.1 8.8 %all-to-all-done.4.refs_0_ = bf16[8,1,2,32,1536]{4,3,2,1,0:T(8,128)(2,1)S(1)} async-done(((bf16[8,1,2,32,1536]{4,3,2,1,0:T(8,128)(2,1)}), bf16[8,1,2,32,1536]{4,3,2,1,0:T(8,128)(2,1)S(1)}, u32[]{:S(2)}, u32[]{:S(2)}) %all-to-all-start.4) | async-done | bytes 1572896 | tf_op jit(solution)/shard_map/all_to_all | solution.py:357
  207.8 6.3 %all-to-all-done.7.refs_5_ = bf16[8,1,2,32,512]{4,3,2,1,0:T(8,128)(2,1)S(1)} async-done(((bf16[8,1,2,32,512]{4,3,2,1,0:T(8,128)(2,1)}), bf16[8,1,2,32,512]{4,3,2,1,0:T(8,128)(2,1)S(1)}, u32[]{:S(2)}, u32[]{:S(2)}) %all-to-all-start.7) | async-done | bytes 524320 | tf_op jit(solution)/shard_map/all_to_all | solution.py:357
  217.8 6.3 %finish_block.12 = bf16[256,2048]{1,0:T(8,128)(2,1)} custom-call(s32[8,4]{1,0:T(8,128)} %fusion.7.refs_0_, bf16[256,1536]{1,0:T(8,128)(2,1)} %get-tuple-element.43.refs_1_, bf16[256,1536]{1,0:T(8,128)(2,1)} %get-tuple-element.44.refs_2_, bf16[256,1536]{1,0:T(8,128)(2,1)} %get-tuple-element.45.refs_3_, bf16[256,1536]{1,0:T(8,128)(2,1)} %get-tuple-element.53.refs_4_, ...), custom_call_target="tpu_custom_call" | custom-call | flops 134217728 | tf_op jit(solution)/shard_map/finish_block/pallas_call | solution.py:39
  230.4 6.4 %finish_block.14 = bf16[256,2048]{1,0:T(8,128)(2,1)} custom-call(s32[8,4]{1,0:T(8,128)} %fusion.7.refs_0_, bf16[256,1536]{1,0:T(8,128)(2,1)} %get-tuple-element.55.refs_1_, bf16[256,1536]{1,0:T(8,128)(2,1)} %get-tuple-element.56.refs_2_, bf16[256,1536]{1,0:T(8,128)(2,1)} %get-tuple-element.57.refs_3_, bf16[256,1536]{1,0:T(8,128)(2,1)} %get-tuple-element.61.refs_4_, ...), custom_call_target="tpu_custom_call" | custom-call | flops 134217728 | tf_op jit(solution)/shard_map/finish_block/pallas_call | solution.py:39
  241.6 11.2 %collective-permute-done.7.refs_7_ = bf16[256,2048]{1,0:T(8,128)(2,1)S(1)} collective-permute-done((bf16[256,2048]{1,0:T(8,128)(2,1)}, bf16[256,2048]{1,0:T(8,128)(2,1)S(1)}, u32[]{:S(2)}, u32[]{:S(2)}) %collective-permute-start.7) | collective-permute-done | bytes 1048608 | tf_op jit(solution)/shard_map/ppermute | solution.py:354
  253.8 6.3 %finish_block.13 = bf16[256,2048]{1,0:T(8,128)(2,1)} custom-call(s32[8,4]{1,0:T(8,128)} %fusion.7.refs_0_, bf16[256,1536]{1,0:T(8,128)(2,1)} %get-tuple-element.43.refs_1_, bf16[256,1536]{1,0:T(8,128)(2,1)} %get-tuple-element.44.refs_2_, bf16[256,1536]{1,0:T(8,128)(2,1)} %get-tuple-element.45.refs_3_, bf16[256,1536]{1,0:T(8,128)(2,1)} %get-tuple-element.53.refs_4_, ...), custom_call_target="tpu_custom_call" | custom-call | flops 134217728 | tf_op jit(solution)/shard_map/finish_block/pallas_call | solution.py:39
  260.7 14.6 %collective-permute-done.10.refs_7_ = bf16[256,2048]{1,0:T(8,128)(2,1)} collective-permute-done((bf16[256,2048]{1,0:T(8,128)(2,1)}, bf16[256,2048]{1,0:T(8,128)(2,1)}, u32[]{:S(2)}, u32[]{:S(2)}) %collective-permute-start.10) | collective-permute-done | bytes 1048608 | tf_op jit(solution)/shard_map/ppermute | solution.py:354
  275.4 6.3 %finish_block.15 = bf16[256,2048]{1,0:T(8,128)(2,1)} custom-call(s32[8,4]{1,0:T(8,128)} %fusion.7.refs_0_, bf16[256,1536]{1,0:T(8,128)(2,1)} %get-tuple-element.55.refs_1_, bf16[256,1536]{1,0:T(8,128)(2,1)} %get-tuple-element.56.refs_2_, bf16[256,1536]{1,0:T(8,128)(2,1)} %get-tuple-element.57.refs_3_, bf16[256,1536]{1,0:T(8,128)(2,1)} %get-tuple-element.61.refs_4_, ...), custom_call_target="tpu_custom_call" | custom-call | flops 134217728 | tf_op jit(solution)/shard_map/finish_block/pallas_call | solution.py:39
  286.9 14.0 %all_to_all.40.refs_5_ = bf16[8,1,2,32,512]{4,3,2,1,0:T(8,128)(2,1)} all-to-all(bf16[8,1,2,32,512]{4,3,2,1,0:T(8,128)(2,1)} %temporal_attention.5), channel_id=1, replica_groups=mesh['seq'=8,'grp'=4] {'seq'}, dimensions={0} | all-to-all | bytes 1048576 | tf_op jit(solution)/shard_map/all_to_all | solution.py:357
  300.8 6.1 %finish_block.8.refs_0_ = bf16[256,2048]{1,0:T(8,128)(2,1)} custom-call(s32[8,4]{1,0:T(8,128)} %fusion.7.refs_0_, bf16[256,1536]{1,0:T(8,128)(2,1)} %get-tuple-element.43.refs_1_, bf16[256,1536]{1,0:T(8,128)(2,1)} %get-tuple-element.44.refs_2_, bf16[256,1536]{1,0:T(8,128)(2,1)} %get-tuple-element.45.refs_3_, bf16[256,1536]{1,0:T(8,128)(2,1)} %get-tuple-element.53.refs_4_, ...), custom_call_target="tpu_custom_call" | custom-call | flops 134217728 | tf_op jit(solution)/shard_map/finish_block/pallas_call | solution.py:39
  306.9 6.1 %finish_block.10.refs_1_ = bf16[256,2048]{1,0:T(8,128)(2,1)} custom-call(s32[8,4]{1,0:T(8,128)} %fusion.7.refs_0_, bf16[256,1536]{1,0:T(8,128)(2,1)} %get-tuple-element.55.refs_1_, bf16[256,1536]{1,0:T(8,128)(2,1)} %get-tuple-element.56.refs_2_, bf16[256,1536]{1,0:T(8,128)(2,1)} %get-tuple-element.57.refs_3_, bf16[256,1536]{1,0:T(8,128)(2,1)} %get-tuple-element.61.refs_4_, ...), custom_call_target="tpu_custom_call" | custom-call | flops 134217728 | tf_op jit(solution)/shard_map/finish_block/pallas_call | solution.py:39
  313.1 6.9 %collective-permute-done.11.refs_3_ = bf16[256,2048]{1,0:T(8,128)(2,1)} collective-permute-done((bf16[256,2048]{1,0:T(8,128)(2,1)}, bf16[256,2048]{1,0:T(8,128)(2,1)}, u32[]{:S(2)}, u32[]{:S(2)}) %collective-permute-start.11) | collective-permute-done | bytes 1048608 | tf_op jit(solution)/shard_map/ppermute | solution.py:354
  319.9 7.7 %combine.1 = bf16[256,2,2048]{2,1,0:T(2,128)(2,1)} custom-call(bf16[256,2,2048]{2,1,0:T(2,128)(2,1)} %t_ref.1, bf16[256,2048]{1,0:T(8,128)(2,1)} %finish_block.8.refs_0_, bf16[256,2048]{1,0:T(8,128)(2,1)} %finish_block.10.refs_1_, bf16[256,2048]{1,0:T(8,128)(2,1)} %copy-done.14, bf16[256,2048]{1,0:T(8,128)(2,1)} %collective-permute-done.11.refs_3_), custom_call_target="tpu_custom_call" | custom-call | tf_op jit(solution)/shard_map/combine/pallas_call | solution.py:326
  (96 shorter events, 77.1 us)
Async XLA Ops:
  6.5 82.0 %all-gather.5.cloned.1.call-start = ((), (), s32[]{:S(2)}) async-start(), calls=%async_computation.8 | async-start | bytes 14155776 | tf_op jit(solution)/shard_map/all_gather | solution.py:363
  9.4 146.0 %all-gather.7.cloned.1.call-start = ((), (), s32[]{:S(2)}) async-start(), calls=%async_computation.9 | async-start | bytes 4718592 | tf_op jit(solution)/shard_map/all_gather | solution.py:368
  13.0 30.1 %copy-start.18 = (s32[8,4]{0,1:T(4,128)S(1)}, s32[8,4]{0,1:T(4,128)}, u32[]{:S(2)}) copy-start(s32[8,4]{0,1:T(4,128)} %param.11) | copy-start | bytes 388
  13.0 30.8 %copy-start.17 = (f32[2,2,4,128]{3,2,1,0:T(4,128)S(1)}, f32[2,2,4,128]{3,2,1,0:T(4,128)}, u32[]{:S(2)}) copy-start(f32[2,2,4,128]{3,2,1,0:T(4,128)} %param.10) | copy-start | bytes 24580
  13.0 30.8 %copy-start.19 = (f32[3]{0:T(128)S(1)}, f32[3]{0:T(128)}, u32[]{:S(2)}) copy-start(f32[3]{0:T(128)} %constant.84.clone) | copy-start | bytes 40
  13.0 29.1 %collective-permute-start = (bf16[256,2048]{1,0:T(8,128)(2,1)S(1)}, bf16[256,2048]{1,0:T(8,128)(2,1)S(1)}, u32[]{:S(2)}, u32[]{:S(2)}) collective-permute-start(bf16[256,2048]{1,0:T(8,128)(2,1)S(1)} %get-tuple-element.70.refs_2_.refs_0_), channel_id=1, source_target_pairs={{0,1},{1,2},{2,3},{3,0},{4,5},{5,6},{6,7},{7,4},{8,9},{9,10},{10,1... | collective-permute-start | bytes 3145736 | tf_op jit(solution)/shard_map/ppermute | solution.py:354
  17.0 47.6 %collective-permute-start.2 = (bf16[256,2048]{1,0:T(8,128)(2,1)}, bf16[256,2048]{1,0:T(8,128)(2,1)S(1)}, u32[]{:S(2)}, u32[]{:S(2)}) collective-permute-start(bf16[256,2048]{1,0:T(8,128)(2,1)} %get-tuple-element.69.refs_3_.refs_1_), channel_id=1, source_target_pairs={{0,1},{1,2},{2,3},{3,0},{4,5},{5,6},{6,7},{7,4},{8,9},{9,10},{10,1... | collective-permute-start | bytes 3145736 | tf_op jit(solution)/shard_map/ppermute | solution.py:354
  43.1 43.1 %collective-permute-start.1 = (bf16[256,2048]{1,0:T(8,128)(2,1)}, bf16[256,2048]{1,0:T(8,128)(2,1)S(1)}, u32[]{:S(2)}, u32[]{:S(2)}) collective-permute-start(bf16[256,2048]{1,0:T(8,128)(2,1)} %get-tuple-element.37.refs_0_), channel_id=1, source_target_pairs={{0,1},{1,2},{2,3},{3,0},{4,5},{5,6},{6,7},{7,4},{8,9},{9,10},{10,1... | collective-permute-start | bytes 3145736 | tf_op jit(solution)/shard_map/ppermute | solution.py:354
  87.2 47.8 %collective-permute-start.4 = (bf16[256,2048]{1,0:T(8,128)(2,1)}, bf16[256,2048]{1,0:T(8,128)(2,1)S(1)}, u32[]{:S(2)}, u32[]{:S(2)}) collective-permute-start(bf16[256,2048]{1,0:T(8,128)(2,1)} %get-tuple-element.39.refs_1_), channel_id=1, source_target_pairs={{0,1},{1,2},{2,3},{3,0},{4,5},{5,6},{6,7},{7,4},{8,9},{9,10},{10,1... | collective-permute-start | bytes 3145736 | tf_op jit(solution)/shard_map/ppermute | solution.py:354
  87.2 48.9 %collective-permute-start.3 = (bf16[256,2048]{1,0:T(8,128)(2,1)}, bf16[256,2048]{1,0:T(8,128)(2,1)}, u32[]{:S(2)}, u32[]{:S(2)}) collective-permute-start(bf16[256,2048]{1,0:T(8,128)(2,1)} %get-tuple-element.40.refs_4_.refs_2_), channel_id=1, source_target_pairs={{0,1},{1,2},{2,3},{3,0},{4,5},{5,6},{6,7},{7,4},{8,9},{9,10},{10,1... | collective-permute-start | bytes 3145736 | tf_op jit(solution)/shard_map/ppermute | solution.py:354
  96.3 30.8 %all-to-all-start = ((bf16[8,1,2,32,1536]{4,3,2,1,0:T(8,128)(2,1)}), bf16[8,1,2,32,1536]{4,3,2,1,0:T(8,128)(2,1)S(1)}, u32[]{:S(2)}, u32[]{:S(2)}) async-start(bf16[8,1,2,32,1536]{4,3,2,1,0:T(8,128)(2,1)} %get-tuple-element.46), calls=%async_computation | async-start | bytes 3145728 | tf_op jit(solution)/shard_map/all_to_all | solution.py:357
  131.6 19.1 %all-to-all-start.3 = ((bf16[8,1,2,32,512]{4,3,2,1,0:T(8,128)(2,1)}), bf16[8,1,2,32,512]{4,3,2,1,0:T(8,128)(2,1)S(1)}, u32[]{:S(2)}, u32[]{:S(2)}) async-start(bf16[8,1,2,32,512]{4,3,2,1,0:T(8,128)(2,1)} %get-tuple-element.58), calls=%async_computation.3 | async-start | bytes 1048576 | tf_op jit(solution)/shard_map/all_to_all | solution.py:357
  136.2 27.4 %collective-permute-start.5 = (bf16[256,2048]{1,0:T(8,128)(2,1)}, bf16[256,2048]{1,0:T(8,128)(2,1)S(1)}, u32[]{:S(2)}, u32[]{:S(2)}) collective-permute-start(bf16[256,2048]{1,0:T(8,128)(2,1)} %get-tuple-element.50.refs_0_), channel_id=1, source_target_pairs={{0,1},{1,2},{2,3},{3,0},{4,5},{5,6},{6,7},{7,4},{8,9},{9,10},{10,1... | collective-permute-start | bytes 3145736 | tf_op jit(solution)/shard_map/ppermute | solution.py:354
  150.6 25.3 %all-to-all-start.6 = ((bf16[8,1,2,32,1536]{4,3,2,1,0:T(8,128)(2,1)}), bf16[8,1,2,32,1536]{4,3,2,1,0:T(8,128)(2,1)S(1)}, u32[]{:S(2)}, u32[]{:S(2)}) async-start(bf16[8,1,2,32,1536]{4,3,2,1,0:T(8,128)(2,1)} %get-tuple-element.63), calls=%async_computation.6 | async-start | bytes 3145728 | tf_op jit(solution)/shard_map/all_to_all | solution.py:357
  176.0 24.9 %all-to-all-start.4 = ((bf16[8,1,2,32,1536]{4,3,2,1,0:T(8,128)(2,1)}), bf16[8,1,2,32,1536]{4,3,2,1,0:T(8,128)(2,1)S(1)}, u32[]{:S(2)}, u32[]{:S(2)}) async-start(bf16[8,1,2,32,1536]{4,3,2,1,0:T(8,128)(2,1)} %get-tuple-element.62), calls=%async_computation.4 | async-start | bytes 3145728 | tf_op jit(solution)/shard_map/all_to_all | solution.py:357
  179.9 37.9 %collective-permute-start.6 = (bf16[256,2048]{1,0:T(8,128)(2,1)}, bf16[256,2048]{1,0:T(8,128)(2,1)}, u32[]{:S(2)}, u32[]{:S(2)}) collective-permute-start(bf16[256,2048]{1,0:T(8,128)(2,1)} %get-tuple-element.67), channel_id=1, source_target_pairs={{0,1},{1,2},{2,3},{3,0},{4,5},{5,6},{6,7},{7,4},{8,9},{9,10},{10,1... | collective-permute-start | bytes 3145736 | tf_op jit(solution)/shard_map/ppermute | solution.py:354
  188.4 42.0 %collective-permute-start.9 = (bf16[256,2048]{1,0:T(8,128)(2,1)}, bf16[256,2048]{1,0:T(8,128)(2,1)}, u32[]{:S(2)}, u32[]{:S(2)}) collective-permute-start(bf16[256,2048]{1,0:T(8,128)(2,1)} %get-tuple-element.68), channel_id=1, source_target_pairs={{0,1},{1,2},{2,3},{3,0},{4,5},{5,6},{6,7},{7,4},{8,9},{9,10},{10,1... | collective-permute-start | bytes 3145736 | tf_op jit(solution)/shard_map/ppermute | solution.py:354
  200.9 13.2 %all-to-all-start.7 = ((bf16[8,1,2,32,512]{4,3,2,1,0:T(8,128)(2,1)}), bf16[8,1,2,32,512]{4,3,2,1,0:T(8,128)(2,1)S(1)}, u32[]{:S(2)}, u32[]{:S(2)}) async-start(bf16[8,1,2,32,512]{4,3,2,1,0:T(8,128)(2,1)} %get-tuple-element.66), calls=%async_computation.7 | async-start | bytes 1048576 | tf_op jit(solution)/shard_map/all_to_all | solution.py:357
  214.1 23.4 %all-to-all-start.5 = ((bf16[8,1,2,32,512]{4,3,2,1,0:T(8,128)(2,1)}), bf16[8,1,2,32,512]{4,3,2,1,0:T(8,128)(2,1)S(1)}, u32[]{:S(2)}, u32[]{:S(2)}) async-start(bf16[8,1,2,32,512]{4,3,2,1,0:T(8,128)(2,1)} %temporal_attention.6), calls=%async_computation.5 | async-start | bytes 1048576 | tf_op jit(solution)/shard_map/all_to_all | solution.py:357
  224.2 28.6 %collective-permute-start.7 = (bf16[256,2048]{1,0:T(8,128)(2,1)}, bf16[256,2048]{1,0:T(8,128)(2,1)S(1)}, u32[]{:S(2)}, u32[]{:S(2)}) collective-permute-start(bf16[256,2048]{1,0:T(8,128)(2,1)} %finish_block.12), channel_id=1, source_target_pairs={{0,1},{1,2},{2,3},{3,0},{4,5},{5,6},{6,7},{7,4},{8,9},{9,10},{10,1... | collective-permute-start | bytes 3145736 | tf_op jit(solution)/shard_map/ppermute | solution.py:354
  236.8 38.6 %collective-permute-start.10 = (bf16[256,2048]{1,0:T(8,128)(2,1)}, bf16[256,2048]{1,0:T(8,128)(2,1)}, u32[]{:S(2)}, u32[]{:S(2)}) collective-permute-start(bf16[256,2048]{1,0:T(8,128)(2,1)} %finish_block.14), channel_id=1, source_target_pairs={{0,1},{1,2},{2,3},{3,0},{4,5},{5,6},{6,7},{7,4},{8,9},{9,10},{10,1... | collective-permute-start | bytes 3145736 | tf_op jit(solution)/shard_map/ppermute | solution.py:354
  237.5 44.9 %all-to-all-start.1 = ((bf16[8,1,2,32,1536]{4,3,2,1,0:T(8,128)(2,1)}), bf16[8,1,2,32,1536]{4,3,2,1,0:T(8,128)(2,1)S(1)}, u32[]{:S(2)}, u32[]{:S(2)}) async-start(bf16[8,1,2,32,1536]{4,3,2,1,0:T(8,128)(2,1)} %get-tuple-element.54), calls=%async_computation.1 | async-start | bytes 3145728 | tf_op jit(solution)/shard_map/all_to_all | solution.py:357
  260.1 53.0 %collective-permute-start.8 = (bf16[256,2048]{1,0:T(8,128)(2,1)}, bf16[256,2048]{1,0:T(8,128)(2,1)S(1)}, u32[]{:S(2)}, u32[]{:S(2)}) collective-permute-start(bf16[256,2048]{1,0:T(8,128)(2,1)} %finish_block.13), channel_id=1, source_target_pairs={{0,1},{1,2},{2,3},{3,0},{4,5},{5,6},{6,7},{7,4},{8,9},{9,10},{10,1... | collective-permute-start | bytes 3145736 | tf_op jit(solution)/shard_map/ppermute | solution.py:354
  281.7 38.2 %collective-permute-start.11 = (bf16[256,2048]{1,0:T(8,128)(2,1)}, bf16[256,2048]{1,0:T(8,128)(2,1)}, u32[]{:S(2)}, u32[]{:S(2)}) collective-permute-start(bf16[256,2048]{1,0:T(8,128)(2,1)} %finish_block.15), channel_id=1, source_target_pairs={{0,1},{1,2},{2,3},{3,0},{4,5},{5,6},{6,7},{7,4},{8,9},{9,10},{10,1... | collective-permute-start | bytes 3145736 | tf_op jit(solution)/shard_map/ppermute | solution.py:354
  (18 other events, 114.1 us)
Sparse Core Ops, SparseCore 0:
  9.5 74.8 all-gather.4
  86.2 46.7 all-gather.6
